TPU v7x, 32 devices: a whole 2x2x4 slice. The times are simulated.
32 devices in a mesh: member: 8 (over y, x, core), region: 4 (over z).
Axes of the slice: x: 2, y: 2, z: 4, core: 2. Of those that a mesh axis runs over, the one named last changes fastest.
Arguments:
- state_prior: bfloat16 [256, 98304], P('member', 'region'), may hold values from -6 to 6
- obs_prior: bfloat16 [256, 8192], P('member', 'region'), may hold values from -6 to 6
- obs_value: float32 [8192], P('region'), may hold values from -12 to 12
- obs_rinv: float32 [8192], P('region'), may hold values from 0.02 to 0.3
- tile_obs: int32 [64, 2048], P('region'), may hold values from 64 to 4031, as said below
- tile_count: int32 [64], P('region'), may hold values from 128 to 2048, as said below
Outputs:
- analysis: bfloat16 [256, 98304], P('member', 'region')
Inputs may be any that keep to these rules, and one draw needn't show every extreme that they name: tile_obs[t] holds each widened position from i * 128 + 128 / 2 to i * 128 + 128 / 2 + 2047 exactly once, for tile i of its region. `tile_count`: each region has a tile with all 2048 slots live.
All inputs are finite; a program needn't handle non-finite values.
Results may differ from a plain program's by a relative error of at most 0.0015.
The roundings to bfloat16 on the way count: a program that leaves them out, or rounds other values in their place, can miss the bound.
Values may be sent and summed in bfloat16 or wider, within the bound.
A program may use at most 128 MiB of HBM per device.

v0:
```python
import functools

import jax
import jax.numpy as jnp
from jax import lax
from jax.experimental import pallas as pl
from jax.experimental.pallas import tpu as pltpu
from jax.sharding import PartitionSpec as P

OBS_TILE = 128
ITERS = 4
RIM = 1024
LOC = 512
CORES = 2
DOUBLINGS = 13
MESH = pl.DeviceIdType.MESH
F32 = jnp.float32
BF16 = jnp.bfloat16


def split(a):
    high = a.astype(BF16)
    return high, (a - high.astype(F32)).astype(BF16)


def mm(a, b):
    return jnp.dot(a, b, preferred_element_type=F32)


def mm_nt(a, b):
    return lax.dot_general(a, b, (((1,), (1,)), ((), ())), preferred_element_type=F32)


def dot3(a, b):
    (ah, al), (bh, bl) = a, b
    return mm(ah, bh) + (mm(ah, bl) + mm(al, bh))


def kernel(
    sizes,
    state, prior, value, rinv, tobs, tcount,
    out,
    pw, vw, rw, yall, xall, res, uh, ul, ev, wt,
    loc_sem, hs_sem, hr_sem, ys_sem, yr_sem, fs_sem, ss_sem, sr_sem, os_sem, or_sem,
):
    groups, regions, rows, per_dev, cells, obs = sizes
    chips = groups // CORES
    members = groups * rows
    me = lax.axis_index("member")
    reg = lax.axis_index("region")
    chip, core = me // CORES, lax.rem(me, CORES)
    sibling = chip * CORES + (CORES - 1 - core)
    wide = obs + 2 * RIM
    width_chip = wide - (chips - 1) * CORES * per_dev * OBS_TILE
    width = width_chip - per_dev * OBS_TILE
    rim_rows = RIM // 128
    obs_rows = obs // 128
    block = per_dev * cells

    def peer(j):
        return lax.rem(me + j, groups)

    barrier = pltpu.get_barrier_semaphore()
    for j in range(1, groups):
        pl.semaphore_signal(barrier, inc=1, device_id={"member": peer(j)}, device_id_type=MESH)

    @pl.when(reg > 0)
    def _():
        pl.semaphore_signal(barrier, inc=1, device_id={"region": reg - 1}, device_id_type=MESH)

    @pl.when(reg < regions - 1)
    def _():
        pl.semaphore_signal(barrier, inc=1, device_id={"region": reg + 1}, device_id_type=MESH)

    own_copies = [
        pltpu.make_async_copy(prior, pw.at[:, pl.ds(RIM, obs)], loc_sem.at[0]),
        pltpu.make_async_copy(value, vw.at[pl.ds(rim_rows, obs_rows), :], loc_sem.at[1]),
        pltpu.make_async_copy(rinv, rw.at[pl.ds(rim_rows, obs_rows), :], loc_sem.at[2]),
    ]
    for copy in own_copies:
        copy.start()

    def state_copy(p, sem_to, sem_from):
        return pltpu.make_async_remote_copy(
            src_ref=state.at[:, pl.ds(pl.multiple_of(p * block, 128), block)],
            dst_ref=xall.at[pl.ds(pl.multiple_of(me * rows, rows), rows), :],
            send_sem=ss_sem.at[sem_to],
            recv_sem=sr_sem.at[sem_from],
            device_id={"member": p},
            device_id_type=MESH,
        )

    own_state = pltpu.make_async_copy(
        state.at[:, pl.ds(pl.multiple_of(me * block, 128), block)],
        xall.at[pl.ds(pl.multiple_of(me * rows, rows), rows), :],
        loc_sem.at[3],
    )
    own_state.start()

    @pl.when(reg == 0)
    def _():
        pw[:, :RIM] = jnp.zeros((rows, RIM), BF16)
        vw[:rim_rows, :] = jnp.zeros((rim_rows, 128), F32)
        rw[:rim_rows, :] = jnp.zeros((rim_rows, 128), F32)

    @pl.when(reg == regions - 1)
    def _():
        pw[:, RIM + obs :] = jnp.zeros((rows, RIM), BF16)
        vw[rim_rows + obs_rows :, :] = jnp.zeros((rim_rows, 128), F32)
        rw[rim_rows + obs_rows :, :] = jnp.zeros((rim_rows, 128), F32)

    expected = groups - 1 + (reg > 0).astype(jnp.int32) + (reg < regions - 1).astype(jnp.int32)
    pl.semaphore_wait(barrier, expected)

    def halo(side):
        at = reg - 1 if side == 0 else reg + 1
        src, dst = (0, RIM + obs) if side == 0 else (obs - RIM, 0)
        src_row, dst_row = src // 128, dst // 128
        made = []
        for n, (a, b) in enumerate(
            (
                (prior.at[:, pl.ds(src, RIM)], pw.at[:, pl.ds(dst, RIM)]),
                (value.at[pl.ds(src_row, rim_rows), :], vw.at[pl.ds(dst_row, rim_rows), :]),
                (rinv.at[pl.ds(src_row, rim_rows), :], rw.at[pl.ds(dst_row, rim_rows), :]),
            )
        ):
            made.append(
                pltpu.make_async_remote_copy(
                    src_ref=a,
                    dst_ref=b,
                    send_sem=hs_sem.at[3 * side + n],
                    recv_sem=hr_sem.at[3 * side + n],
                    device_id={"region": at},
                    device_id_type=MESH,
                )
            )
        return made

    @pl.when(reg > 0)
    def _():
        for copy in halo(0):
            copy.start()

    @pl.when(reg < regions - 1)
    def _():
        for copy in halo(1):
            copy.start()

    state_copy(sibling, 0, me).start()
    for copy in own_copies:
        copy.wait()

    @pl.when(reg < regions - 1)
    def _():
        for copy in halo(0):
            copy.wait_recv()

    @pl.when(reg > 0)
    def _():
        for copy in halo(1):
            copy.wait_recv()

    def window(c):
        return pw.at[:, pl.ds(pl.multiple_of(c * (CORES * per_dev * OBS_TILE), 128), width_chip)]

    def yrows(m):
        return yall.at[pl.ds(pl.multiple_of(m * rows, rows), rows), :]

    def prior_copy(src, source, to, send_sem):
        return pltpu.make_async_remote_copy(
            src_ref=src,
            dst_ref=yrows(source),
            send_sem=send_sem,
            recv_sem=yr_sem.at[source],
            device_id={"member": to},
            device_id_type=MESH,
        )

    sends = []
    for j in range(1, chips):
        c = lax.rem(chip + j, chips)
        sends.append(prior_copy(window(c), me, c * CORES + core, ys_sem.at[j]))
    sends.append(prior_copy(window(chip), me, sibling, ys_sem.at[0]))
    for copy in sends:
        copy.start()
    own_prior = pltpu.make_async_copy(window(chip), yrows(me), loc_sem.at[0])
    own_prior.start()

    pos0 = me * (per_dev * OBS_TILE)
    nrow = width // 128
    hpad = (nrow + 15) // 16 * 16
    slots = tobs.shape[1]
    first = me * per_dev
    lane = lax.broadcasted_iota(jnp.int32, (1, slots), 1)
    hi_iota = lax.broadcasted_iota(jnp.int32, (hpad, slots), 0)
    lo_iota = lax.broadcasted_iota(jnp.int32, (128, slots), 0)
    base = per_dev * me
    value_row = jnp.concatenate([vw[pl.ds(base + h, 1), :] for h in range(nrow)], axis=1)
    rinv_row = jnp.concatenate([rw[pl.ds(base + h, 1), :] for h in range(nrow)], axis=1)
    place = lax.broadcasted_iota(jnp.int32, (1, width), 1)
    weights = []
    for t in range(per_dev):
        rel = tobs[pl.ds(first + t, 1), :] - pos0
        live = lane < tcount[first + t]
        hi = jnp.where(live, rel // 128, -1)
        lo = lax.rem(rel, 128)
        one_hi = jnp.where(hi_iota == hi, 1.0, 0.0).astype(BF16)
        one_lo = jnp.where(lo_iota == lo, 1.0, 0.0).astype(BF16)
        grid = mm_nt(one_hi, one_lo)
        mask = jnp.concatenate([grid[h : h + 1, :] for h in range(nrow)], axis=1)
        dist = jnp.abs(place - (RIM + t * OBS_TILE + OBS_TILE // 2)).astype(F32) / LOC
        weights.append(jnp.sqrt(mask * rinv_row / (1.0 + dist * dist)))

    for j in range(1, chips):
        c = lax.rem(chip + j, chips)
        source = c * CORES + core
        prior_copy(yrows(source), source, sibling, fs_sem.at[j]).wait_recv()
        prior_copy(yrows(source), source, sibling, fs_sem.at[j]).start()
    for copy in sends:
        copy.wait_send()
    for j in range(1, groups):
        p = peer(j)

        @pl.when(p != sibling)
        def _():
            state_copy(p, j, me).start()

    for j in range(chips):
        c = lax.rem(chip + j, chips)
        source = c * CORES + (CORES - 1 - core)
        prior_copy(yrows(source), source, sibling, fs_sem.at[0]).wait_recv()
    own_prior.wait()

    offset = core * (per_dev * OBS_TILE)
    chunk = 256
    sums = [jnp.zeros((members, 128), F32) for _ in range(per_dev)]
    for k in range(width // chunk):
        y = yall[:, pl.ds(pl.multiple_of(offset + k * chunk, 128), chunk)].astype(F32)
        ybar = jnp.sum(y, axis=0, keepdims=True) * (1.0 / members)
        pert = y - ybar
        dep = value_row[:, k * chunk : (k + 1) * chunk] - ybar
        for t in range(per_dev):
            root = weights[t][:, k * chunk : (k + 1) * chunk]
            u = pert * root
            high, low = split(u)
            uh[t, :, k * chunk : (k + 1) * chunk] = high
            ul[t, :, k * chunk : (k + 1) * chunk] = low
            v = u * (root * dep)
            for q in range(chunk // 128):
                sums[t] = sums[t] + v[:, q * 128 : (q + 1) * 128]

    row_i = lax.broadcasted_iota(jnp.int32, (members, members), 0)
    col_i = lax.broadcasted_iota(jnp.int32, (members, members), 1)
    eye = jnp.where(row_i == col_i, 1.0, 0.0).astype(F32)
    scales, zs = [], []
    for t in range(per_dev):
        cross = mm_nt(uh[t], ul[t])
        amat = (members - 1.0) * eye + mm_nt(uh[t], uh[t]) + (cross + cross.T)
        mmat = amat * (1.0 / (members - 1.0))
        scale = jnp.sqrt(jnp.sum(jnp.sum(mmat * mmat, axis=0, keepdims=True), axis=1, keepdims=True))
        y = mmat / scale
        m = 1.5 * eye - 0.5 * y
        z = m
        zp, yp, mp = split(z), split(y), split(m)
        for step in range(1, ITERS + 1):
            yp = split(dot3(yp, mp))
            if step > 1:
                z = dot3(mp, zp)
                zp = split(z)
            p = dot3(zp, yp)
            if step < ITERS:
                mp = split(1.5 * eye - 0.5 * p)
        rhs = jnp.broadcast_to(jnp.sum(sums[t], axis=1, keepdims=True), (members, 128))
        ev[t, :, :members] = eye - p
        ev[t, :, members:] = dot3(zp, split(rhs))
        scales.append(scale)
        zs.append((z, zp))

    def doubling(step, carry):
        for t in range(per_dev):
            e = split(ev[t, :, :members])
            v = ev[t, :, members:]
            ev[t, :, members:] = v + dot3(e, split(v))
            ev[t, :, :members] = dot3(e, e)
        return carry

    lax.fori_loop(0, DOUBLINGS, doubling, 0)
    for t in range(per_dev):
        z, zp = zs[t]
        wmean = dot3(zp, split(ev[t, :, members:])) / (scales[t] * (members - 1.0))
        wide_mean = jnp.concatenate([wmean] * (members // 128), axis=1)
        wt[t] = (z / jnp.sqrt(scales[t]) + wide_mean).T.astype(BF16)

    own_state.wait()
    for j in range(1, groups):
        p = peer(j)
        state_copy(p, j, p).wait_recv()

    def result_copy(p, j, t, sem_from):
        return pltpu.make_async_remote_copy(
            src_ref=res.at[pl.ds(pl.multiple_of(p * rows, rows), rows), pl.ds(t * cells, cells)],
            dst_ref=out.at[:, pl.ds(pl.multiple_of(me * block + t * cells, 128), cells)],
            send_sem=os_sem.at[j, t],
            recv_sem=or_sem.at[sem_from, t],
            device_id={"member": p},
            device_id_type=MESH,
        )

    def own_result(t):
        return pltpu.make_async_copy(
            res.at[pl.ds(pl.multiple_of(me * rows, rows), rows), pl.ds(t * cells, cells)],
            out.at[:, pl.ds(pl.multiple_of(me * block + t * cells, 128), cells)],
            loc_sem.at[1 + t],
        )

    for t in range(per_dev):

        def columns(n, carry):
            at = pl.ds(pl.multiple_of(t * cells + n * chunk, 128), chunk)
            x = xall[:, at].astype(F32)
            xbar = jnp.sum(x, axis=0, keepdims=True) * (1.0 / members)
            pert = (x - xbar).astype(BF16)
            res[:, at] = (xbar + mm(wt[t], pert)).astype(BF16)
            return carry

        lax.fori_loop(0, cells // chunk, columns, 0)
        for j in range(1, groups):
            result_copy(peer(j), j, t, me).start()
        own_result(t).start()

    for t in range(per_dev):
        own_result(t).wait()
        for j in range(1, groups):
            result_copy(peer(j), j, t, me).wait_send()
        for j in range(1, groups):
            p = peer(j)
            result_copy(p, j, t, p).wait_recv()
    for j in range(1, groups):
        p = peer(j)

        @pl.when(p != sibling)
        def _():
            state_copy(p, j, me).wait_send()

    state_copy(sibling, 0, me).wait_send()
    for j in range(1, chips):
        c = lax.rem(chip + j, chips)
        source = c * CORES + core
        prior_copy(yrows(source), source, sibling, fs_sem.at[j]).wait_send()

    @pl.when(reg > 0)
    def _():
        for copy in halo(0):
            copy.wait_send()

    @pl.when(reg < regions - 1)
    def _():
        for copy in halo(1):
            copy.wait_send()


def body(groups, regions, state_prior, obs_prior, obs_value, obs_rinv, tile_obs, tile_count):
    rows = state_prior.shape[0]
    tiles = tile_obs.shape[0]
    per_dev = tiles // groups
    cells = state_prior.shape[1] // tiles
    obs = obs_prior.shape[1]
    members = groups * rows
    chips = groups // CORES
    width_chip = obs + 2 * RIM - (chips - 1) * CORES * per_dev * OBS_TILE
    width = width_chip - per_dev * OBS_TILE
    sizes = (groups, regions, rows, per_dev, cells, obs)
    dma = pltpu.SemaphoreType.DMA
    return pl.pallas_call(
        functools.partial(kernel, sizes),
        out_shape=jax.ShapeDtypeStruct(state_prior.shape, state_prior.dtype),
        in_specs=[pl.BlockSpec(memory_space=pl.ANY)] * 4
        + [pl.BlockSpec(memory_space=pltpu.VMEM), pl.BlockSpec(memory_space=pltpu.SMEM)],
        out_specs=pl.BlockSpec(memory_space=pl.ANY),
        scratch_shapes=[
            pltpu.VMEM((rows, obs + 2 * RIM), BF16),
            pltpu.VMEM(((obs + 2 * RIM) // 128, 128), F32),
            pltpu.VMEM(((obs + 2 * RIM) // 128, 128), F32),
            pltpu.VMEM((members, width_chip), BF16),
            pltpu.VMEM((members, per_dev * cells), BF16),
            pltpu.VMEM((members, per_dev * cells), BF16),
            pltpu.VMEM((per_dev, members, width), BF16),
            pltpu.VMEM((per_dev, members, width), BF16),
            pltpu.VMEM((per_dev, members, members + 128), F32),
            pltpu.VMEM((per_dev, members, members), BF16),
            dma((4,)),
            dma((6,)),
            dma((6,)),
            dma((chips,)),
            dma((groups,)),
            dma((chips,)),
            dma((groups,)),
            dma((groups,)),
            dma((groups, per_dev)),
            dma((groups, per_dev)),
        ],
        compiler_params=pltpu.CompilerParams(
            collective_id=0, has_side_effects=True, vmem_limit_bytes=40 * 1024 * 1024
        ),
        cost_estimate=pl.CostEstimate(flops=4_000_000_000, bytes_accessed=8_000_000, transcendentals=0),
    )(
        state_prior,
        obs_prior,
        obs_value.reshape(-1, 128),
        obs_rinv.reshape(-1, 128),
        tile_obs,
        tile_count,
    )


def solution(mesh):
    placed = (
        P("member", "region"),
        P("member", "region"),
        P("region"),
        P("region"),
        P("region", None),
        P("region"),
    )
    return jax.shard_map(
        functools.partial(body, mesh.shape["member"], mesh.shape["region"]),
        mesh=mesh,
        in_specs=placed,
        out_specs=P("member", "region"),
        check_vma=False,
    )
```

profile of v0, /device:TPU:1, one launch (start us, length us, event | category | flops | bytes accessed | tf_op | source)
XLA Modules:
  0.0 60.7 jit_solution(12980275694628569325)
XLA Ops:
  0.0 0.0 copy-start
  0.0 1.4 %copy-done = bf16[32,24576]{1,0:T(8,128)(2,1)S(1)} copy-done((bf16[32,24576]{1,0:T(8,128)(2,1)S(1)}, bf16[32,24576]{1,0:T(8,128)(2,1)}, u32[]{:S(2)}) %copy-start) | copy-done | bytes 1572888
  1.4 0.0 copy-start.1
  1.4 0.9 %copy-done.1 = bf16[32,2048]{1,0:T(8,128)(2,1)S(1)} copy-done((bf16[32,2048]{1,0:T(8,128)(2,1)S(1)}, bf16[32,2048]{1,0:T(8,128)(2,1)}, u32[]{:S(2)}) %copy-start.1) | copy-done | bytes 131096
  2.3 0.0 copy-start.2
  2.3 0.9 %copy-done.2 = s32[16,2048]{1,0:T(8,128)S(1)} copy-done((s32[16,2048]{1,0:T(8,128)S(1)}, s32[16,2048]{1,0:T(8,128)}, u32[]{:S(2)}) %copy-start.2) | copy-done | bytes 131096
  3.2 0.0 copy-start.3
  3.2 0.7 %copy-done.3 = f32[2048]{0:T(1024)S(1)} copy-done((f32[2048]{0:T(1024)S(1)}, f32[2048]{0:T(1024)}, u32[]{:S(2)}) %copy-start.3) | copy-done | bytes 8216
  3.9 0.0 copy-start.4
  3.9 0.7 %copy-done.4 = f32[2048]{0:T(1024)S(1)} copy-done((f32[2048]{0:T(1024)S(1)}, f32[2048]{0:T(1024)}, u32[]{:S(2)}) %copy-start.4) | copy-done | bytes 8216
  4.6 0.0 copy-start.5
  4.6 0.7 %copy-done.5 = s32[16]{0:T(128)S(1)} copy-done((s32[16]{0:T(128)S(1)}, s32[16]{0:T(128)}, u32[]{:S(2)}) %copy-start.5) | copy-done | bytes 88
  5.3 54.3 %shard_map.64 = bf16[32,24576]{1,0:T(8,128)(2,1)S(1)} custom-call(bf16[32,24576]{1,0:T(8,128)(2,1)S(1)} %copy-done, bf16[32,2048]{1,0:T(8,128)(2,1)S(1)} %copy-done.1, f32[16,128]{1,0:T(8,128)S(1)} %bitcast.2, f32[16,128]{1,0:T(8,128)S(1)} %bitcast.3, s32[16,2048]{1,0:T(8,128)S(1)} %copy-done.2, s32[16]{0:T(128)S(1)} %copy-done.5), custom_call_target="tpu_custom_call" | custom-call | flops 4000000000 | bytes 8000000 | tf_op jit(solution)/shard_map/pallas_call | solution.py:374
  59.6 1.1 %copy.8 = bf16[32,24576]{1,0:T(8,128)(2,1)} copy(bf16[32,24576]{1,0:T(8,128)(2,1)S(1)} %shard_map.64) | data formatting | bytes 3145728
Async XLA Ops:
  0.0 1.4 %copy-start = (bf16[32,24576]{1,0:T(8,128)(2,1)S(1)}, bf16[32,24576]{1,0:T(8,128)(2,1)}, u32[]{:S(2)}) copy-start(bf16[32,24576]{1,0:T(8,128)(2,1)} %state.1) | copy-start | bytes 4718596
  1.4 0.9 %copy-start.1 = (bf16[32,2048]{1,0:T(8,128)(2,1)S(1)}, bf16[32,2048]{1,0:T(8,128)(2,1)}, u32[]{:S(2)}) copy-start(bf16[32,2048]{1,0:T(8,128)(2,1)} %prior.1) | copy-start | bytes 393220
  2.3 0.9 %copy-start.2 = (s32[16,2048]{1,0:T(8,128)S(1)}, s32[16,2048]{1,0:T(8,128)}, u32[]{:S(2)}) copy-start(s32[16,2048]{1,0:T(8,128)} %tobs.1) | copy-start | bytes 393220
  3.2 0.7 %copy-start.3 = (f32[2048]{0:T(1024)S(1)}, f32[2048]{0:T(1024)}, u32[]{:S(2)}) copy-start(f32[2048]{0:T(1024)} %param.8) | copy-start | bytes 24580
  3.9 0.7 %copy-start.4 = (f32[2048]{0:T(1024)S(1)}, f32[2048]{0:T(1024)}, u32[]{:S(2)}) copy-start(f32[2048]{0:T(1024)} %param.9) | copy-start | bytes 24580
  4.6 0.7 %copy-start.5 = (s32[16]{0:T(128)S(1)}, s32[16]{0:T(128)}, u32[]{:S(2)}) copy-start(s32[16]{0:T(128)} %tcount.1) | copy-start | bytes 196
where the time goes:
time: 61 us; the launch traced here: 60.7 us
  Pallas kernels  54.3 us (89%)
  local copies, waits for them, and re-layouts  6.41 us (11%)
    pallas_call x1, Pallas kernels, body(): pl.pallas_call(functools.partial(kernel, sizes), out_shape=jax.ShapeDtype...  54.3 us
    unnamed x13, local copies, waits for them, and re-layouts  6.41 us

commit v1 on v0

--- a/solution.py
+++ b/solution.py
@@ -2,6 +2,7 @@
 
 import jax
 import jax.numpy as jnp
+import numpy as np
 from jax import lax
 from jax.experimental import pallas as pl
 from jax.experimental.pallas import tpu as pltpu
@@ -12,7 +13,9 @@
 RIM = 1024
 LOC = 512
 CORES = 2
-DOUBLINGS = 13
+VALUE_MAX = 6.0
+RINV_MAX = 0.3
+SLOTS_HALF = 1024
 MESH = pl.DeviceIdType.MESH
 F32 = jnp.float32
 BF16 = jnp.bfloat16
@@ -33,14 +36,27 @@
 
 def dot3(a, b):
     (ah, al), (bh, bl) = a, b
-    return mm(ah, bh) + (mm(ah, bl) + mm(al, bh))
+    return mm(jnp.concatenate([ah, ah, al], axis=1), jnp.concatenate([bh, bl, bh], axis=0))
+
+
+def factors(members):
+    apart = np.arange(-SLOTS_HALF, SLOTS_HALF) / LOC
+    trace = RINV_MAX * np.sum(1.0 / (1.0 + apart * apart)) * members * VALUE_MAX**2
+    low = 0.9 * (members - 1.0) / ((members - 1.0) * np.sqrt(members) + trace)
+    scales = []
+    while True:
+        scales.append(float(2.0 / (1.0 + low)))
+        rest = ((1.0 - low) / (1.0 + low)) ** 2
+        if rest < 1e-7:
+            return scales
+        low = 1.0 - rest
 
 
 def kernel(
     sizes,
     state, prior, value, rinv, tobs, tcount,
     out,
-    pw, vw, rw, yall, xall, res, uh, ul, ev, wt,
+    pw, vw, rw, tv, ts, yall, xall, res, uh, ul, wt,
     loc_sem, hs_sem, hr_sem, ys_sem, yr_sem, fs_sem, ss_sem, sr_sem, os_sem, or_sem,
 ):
     groups, regions, rows, per_dev, cells, obs = sizes
@@ -76,19 +92,24 @@
         pltpu.make_async_copy(prior, pw.at[:, pl.ds(RIM, obs)], loc_sem.at[0]),
         pltpu.make_async_copy(value, vw.at[pl.ds(rim_rows, obs_rows), :], loc_sem.at[1]),
         pltpu.make_async_copy(rinv, rw.at[pl.ds(rim_rows, obs_rows), :], loc_sem.at[2]),
+        pltpu.make_async_copy(tobs, tv, loc_sem.at[4]),
+        pltpu.make_async_copy(tcount, ts, loc_sem.at[5]),
     ]
     for copy in own_copies:
         copy.start()
 
-    def state_copy(p, sem_to, sem_from):
+    def state_copy(p, j, t, source):
         return pltpu.make_async_remote_copy(
-            src_ref=state.at[:, pl.ds(pl.multiple_of(p * block, 128), block)],
-            dst_ref=xall.at[pl.ds(pl.multiple_of(me * rows, rows), rows), :],
-            send_sem=ss_sem.at[sem_to],
-            recv_sem=sr_sem.at[sem_from],
+            src_ref=state.at[:, pl.ds(pl.multiple_of(p * block + t * cells, 128), cells)],
+            dst_ref=xall.at[pl.ds(pl.multiple_of(me * rows, rows), rows), pl.ds(t * cells, cells)],
+            send_sem=ss_sem.at[j, t],
+            recv_sem=sr_sem.at[source, t],
             device_id={"member": p},
             device_id_type=MESH,
         )
+
+    def across(j):
+        return lax.rem(chip + j, chips) * CORES + core, CORES * j
 
     own_state = pltpu.make_async_copy(
         state.at[:, pl.ds(pl.multiple_of(me * block, 128), block)],
@@ -146,7 +167,11 @@
         for copy in halo(1):
             copy.start()
 
-    state_copy(sibling, 0, me).start()
+    for t in range(per_dev):
+        state_copy(sibling, 0, t, me).start()
+    for j in range(1, chips):
+        p, far = across(j)
+        state_copy(p, far, 0, me).start()
     for copy in own_copies:
         copy.wait()
 
@@ -200,8 +225,8 @@
     place = lax.broadcasted_iota(jnp.int32, (1, width), 1)
     weights = []
     for t in range(per_dev):
-        rel = tobs[pl.ds(first + t, 1), :] - pos0
-        live = lane < tcount[first + t]
+        rel = tv[pl.ds(first + t, 1), :] - pos0
+        live = lane < ts[first + t]
         hi = jnp.where(live, rel // 128, -1)
         lo = lax.rem(rel, 128)
         one_hi = jnp.where(hi_iota == hi, 1.0, 0.0).astype(BF16)
@@ -218,12 +243,16 @@
         prior_copy(yrows(source), source, sibling, fs_sem.at[j]).start()
     for copy in sends:
         copy.wait_send()
-    for j in range(1, groups):
-        p = peer(j)
-
-        @pl.when(p != sibling)
-        def _():
-            state_copy(p, j, me).start()
+    def other(j):
+        return lax.rem(chip + j, chips) * CORES + (CORES - 1 - core), CORES * j + 1
+
+    for j in range(1, chips):
+        p, far = other(j)
+        state_copy(p, far, 0, me).start()
+    for t in range(1, per_dev):
+        for j in range(1, chips):
+            for p, far in (across(j), other(j)):
+                state_copy(p, far, t, me).start()
 
     for j in range(chips):
         c = lax.rem(chip + j, chips)
@@ -233,68 +262,64 @@
 
     offset = core * (per_dev * OBS_TILE)
     chunk = 256
-    sums = [jnp.zeros((members, 128), F32) for _ in range(per_dev)]
     for k in range(width // chunk):
+        at = slice(k * chunk, (k + 1) * chunk)
         y = yall[:, pl.ds(pl.multiple_of(offset + k * chunk, 128), chunk)].astype(F32)
         ybar = jnp.sum(y, axis=0, keepdims=True) * (1.0 / members)
         pert = y - ybar
-        dep = value_row[:, k * chunk : (k + 1) * chunk] - ybar
+        dep = value_row[:, at] - ybar
         for t in range(per_dev):
-            root = weights[t][:, k * chunk : (k + 1) * chunk]
-            u = pert * root
-            high, low = split(u)
-            uh[t, :, k * chunk : (k + 1) * chunk] = high
-            ul[t, :, k * chunk : (k + 1) * chunk] = low
-            v = u * (root * dep)
-            for q in range(chunk // 128):
-                sums[t] = sums[t] + v[:, q * 128 : (q + 1) * 128]
+            root = weights[t][:, at]
+            high, low = split(pert * root)
+            uh[t, :members, at] = high
+            ul[t, :, at] = low
+            scaled = jnp.broadcast_to(root * dep, (8, chunk))
+            rough = scaled.astype(BF16).astype(F32)
+            uh[t, members:, at] = jnp.concatenate([rough, scaled - rough], axis=0).astype(BF16)
 
     row_i = lax.broadcasted_iota(jnp.int32, (members, members), 0)
     col_i = lax.broadcasted_iota(jnp.int32, (members, members), 1)
     eye = jnp.where(row_i == col_i, 1.0, 0.0).astype(F32)
-    scales, zs = [], []
-    for t in range(per_dev):
-        cross = mm_nt(uh[t], ul[t])
-        amat = (members - 1.0) * eye + mm_nt(uh[t], uh[t]) + (cross + cross.T)
+    tiles = range(per_dev)
+    cs = factors(members)
+    scales, ps, es, vs = [], [], [], []
+    main = [mm_nt(uh[t], uh[t, :members, :]) for t in tiles]
+    cross = [mm_nt(uh[t], ul[t]) for t in tiles]
+    for t in tiles:
+        half = cross[t][:members]
+        amat = (members - 1.0) * eye + main[t][:members] + (half + half.T)
         mmat = amat * (1.0 / (members - 1.0))
         scale = jnp.sqrt(jnp.sum(jnp.sum(mmat * mmat, axis=0, keepdims=True), axis=1, keepdims=True))
-        y = mmat / scale
-        m = 1.5 * eye - 0.5 * y
-        z = m
-        zp, yp, mp = split(z), split(y), split(m)
-        for step in range(1, ITERS + 1):
-            yp = split(dot3(yp, mp))
-            if step > 1:
-                z = dot3(mp, zp)
-                zp = split(z)
-            p = dot3(zp, yp)
-            if step < ITERS:
-                mp = split(1.5 * eye - 0.5 * p)
-        rhs = jnp.broadcast_to(jnp.sum(sums[t], axis=1, keepdims=True), (members, 128))
-        ev[t, :, :members] = eye - p
-        ev[t, :, members:] = dot3(zp, split(rhs))
+        rhs = main[t][members : members + 1] + main[t][members + 8 : members + 9] + cross[t][members : members + 1]
         scales.append(scale)
-        zs.append((z, zp))
-
-    def doubling(step, carry):
-        for t in range(per_dev):
-            e = split(ev[t, :, :members])
-            v = ev[t, :, members:]
-            ev[t, :, members:] = v + dot3(e, split(v))
-            ev[t, :, :members] = dot3(e, e)
-        return carry
-
-    lax.fori_loop(0, DOUBLINGS, doubling, 0)
-    for t in range(per_dev):
-        z, zp = zs[t]
-        wmean = dot3(zp, split(ev[t, :, members:])) / (scales[t] * (members - 1.0))
-        wide_mean = jnp.concatenate([wmean] * (members // 128), axis=1)
-        wt[t] = (z / jnp.sqrt(scales[t]) + wide_mean).T.astype(BF16)
+        ps.append(mmat / scale)
+        vs.append(jnp.broadcast_to(rhs * (float(np.prod(cs)) / (members - 1.0)) / scale, (16, members)))
+        es.append(eye - cs[0] * ps[t])
+
+    zs = [1.5 * eye - 0.5 * ps[t] for t in tiles]
+    squares = [None for t in tiles]
+    for level in range(max(len(cs), 2 * ITERS)):
+        for t in tiles:
+            if level < len(cs) - 1:
+                e = split(es[t])
+                v = split(vs[t])
+                both = dot3(tuple(jnp.concatenate(x, axis=0) for x in zip(e, v)), e)
+                vs[t] = vs[t] + both[members:]
+                es[t] = (1.0 - cs[level + 1]) * eye + cs[level + 1] * both[:members]
+            elif level == len(cs) - 1:
+                vs[t] = vs[t] + dot3(split(vs[t]), split(es[t]))
+            if level < 2 * ITERS - 2:
+                if level % 2 == 0:
+                    p = split(ps[t])
+                    squares[t] = dot3(p, p)
+                else:
+                    ps[t] = 2.25 * ps[t] + dot3(split(squares[t]), split(0.25 * ps[t] - 1.5 * eye))
+            if level >= 2 and level % 2 == 0 and level <= 2 * ITERS - 2:
+                zs[t] = dot3(split(zs[t]), split(1.5 * eye - 0.5 * ps[t]))
+    for t in tiles:
+        wt[t] = (zs[t] / jnp.sqrt(scales[t]) + vs[t][:1]).astype(BF16)
 
     own_state.wait()
-    for j in range(1, groups):
-        p = peer(j)
-        state_copy(p, j, p).wait_recv()
 
     def result_copy(p, j, t, sem_from):
         return pltpu.make_async_remote_copy(
@@ -314,6 +339,9 @@
         )
 
     for t in range(per_dev):
+        for j in range(1, groups):
+            p = peer(j)
+            state_copy(p, j, t, p).wait_recv()
 
         def columns(n, carry):
             at = pl.ds(pl.multiple_of(t * cells + n * chunk, 128), chunk)
@@ -335,14 +363,11 @@
         for j in range(1, groups):
             p = peer(j)
             result_copy(p, j, t, p).wait_recv()
-    for j in range(1, groups):
-        p = peer(j)
-
-        @pl.when(p != sibling)
-        def _():
-            state_copy(p, j, me).wait_send()
-
-    state_copy(sibling, 0, me).wait_send()
+    for t in range(per_dev):
+        state_copy(sibling, 0, t, me).wait_send()
+        for j in range(1, chips):
+            for p, far in (across(j), other(j)):
+                state_copy(p, far, t, me).wait_send()
     for j in range(1, chips):
         c = lax.rem(chip + j, chips)
         source = c * CORES + core
@@ -374,33 +399,33 @@
     return pl.pallas_call(
         functools.partial(kernel, sizes),
         out_shape=jax.ShapeDtypeStruct(state_prior.shape, state_prior.dtype),
-        in_specs=[pl.BlockSpec(memory_space=pl.ANY)] * 4
-        + [pl.BlockSpec(memory_space=pltpu.VMEM), pl.BlockSpec(memory_space=pltpu.SMEM)],
+        in_specs=[pl.BlockSpec(memory_space=pl.ANY)] * 6,
         out_specs=pl.BlockSpec(memory_space=pl.ANY),
         scratch_shapes=[
             pltpu.VMEM((rows, obs + 2 * RIM), BF16),
             pltpu.VMEM(((obs + 2 * RIM) // 128, 128), F32),
             pltpu.VMEM(((obs + 2 * RIM) // 128, 128), F32),
+            pltpu.VMEM(tile_obs.shape, jnp.int32),
+            pltpu.SMEM(tile_count.shape, jnp.int32),
             pltpu.VMEM((members, width_chip), BF16),
             pltpu.VMEM((members, per_dev * cells), BF16),
             pltpu.VMEM((members, per_dev * cells), BF16),
+            pltpu.VMEM((per_dev, members + 16, width), BF16),
             pltpu.VMEM((per_dev, members, width), BF16),
-            pltpu.VMEM((per_dev, members, width), BF16),
-            pltpu.VMEM((per_dev, members, members + 128), F32),
             pltpu.VMEM((per_dev, members, members), BF16),
-            dma((4,)),
+            dma((6,)),
             dma((6,)),
             dma((6,)),
             dma((chips,)),
             dma((groups,)),
             dma((chips,)),
-            dma((groups,)),
-            dma((groups,)),
+            dma((groups, per_dev)),
+            dma((groups, per_dev)),
             dma((groups, per_dev)),
             dma((groups, per_dev)),
         ],
         compiler_params=pltpu.CompilerParams(
-            collective_id=0, has_side_effects=True, vmem_limit_bytes=40 * 1024 * 1024
+            collective_id=0, has_side_effects=True, vmem_limit_bytes=62 * 1024 * 1024
         ),
         cost_estimate=pl.CostEstimate(flops=4_000_000_000, bytes_accessed=8_000_000, transcendentals=0),
     )(

time: 61 us -> 52.1 us (0.85)
  Pallas kernels: 54.3 us -> 49.3 us
  local copies, waits for them, and re-layouts: 6.41 us -> 2.65 us
    pallas_call x1, Pallas kernels: 54.3 us -> 49.3 us  [body(): pl.pallas_call(functools.partial(kernel, sizes), out_shape=jax.ShapeDtype...]
    unnamed x13 -> x1, local copies, waits for them, and re-layouts: 6.41 us -> 2.65 us
where the time goes in v1:
time: 52.1 us; the launch traced here: 52 us
  Pallas kernels  49.3 us (95%)
  local copies, waits for them, and re-layouts  2.65 us (5%)
    pallas_call x1, Pallas kernels, body(): pl.pallas_call(functools.partial(kernel, sizes), out_shape=jax.ShapeDtype...  49.3 us
    unnamed x1, local copies, waits for them, and re-layouts  2.65 us

profile of v1, /device:TPU:1, one launch (start us, length us, event | category | flops | bytes accessed | tf_op | source)
XLA Modules:
  0.0 52.0 jit_solution(664170270968177429)
XLA Ops:
  0.0 49.3 %shard_map.64 = bf16[32,24576]{1,0:T(8,128)(2,1)} custom-call(bf16[32,24576]{1,0:T(8,128)(2,1)} %state.1, bf16[32,2048]{1,0:T(8,128)(2,1)} %prior.1, f32[16,128]{1,0:T(8,128)} %bitcast.2, f32[16,128]{1,0:T(8,128)} %bitcast.3, s32[16,2048]{1,0:T(8,128)} %tobs.1, s32[16]{0:T(128)} %tcount.1), custom_call_target="tpu_custom_call" | custom-call | flops 4000000000 | bytes 8000000 | tf_op jit(solution)/shard_map/pallas_call | solution.py:399
  49.3 2.7 %copy.8 = bf16[32,24576]{1,0:T(8,128)(2,1)} copy(bf16[32,24576]{1,0:T(8,128)(2,1)} %shard_map.64) | data formatting | bytes 3145728

commit v2 on v1

--- a/solution.py
+++ b/solution.py
@@ -16,6 +16,7 @@
 VALUE_MAX = 6.0
 RINV_MAX = 0.3
 SLOTS_HALF = 1024
+PIECE = 512
 MESH = pl.DeviceIdType.MESH
 F32 = jnp.float32
 BF16 = jnp.bfloat16
@@ -56,8 +57,8 @@
     sizes,
     state, prior, value, rinv, tobs, tcount,
     out,
-    pw, vw, rw, tv, ts, yall, xall, res, uh, ul, wt,
-    loc_sem, hs_sem, hr_sem, ys_sem, yr_sem, fs_sem, ss_sem, sr_sem, os_sem, or_sem,
+    pw, vw, rw, tv, ts, roots, values, yall, xall, res, uh, ul, wt,
+    loc_sem, own_sem, hs_sem, hr_sem, ys_sem, yr_sem, fs_sem, ss_sem, sr_sem, os_sem, or_sem,
 ):
     groups, regions, rows, per_dev, cells, obs = sizes
     chips = groups // CORES
@@ -68,7 +69,7 @@
     sibling = chip * CORES + (CORES - 1 - core)
     wide = obs + 2 * RIM
     width_chip = wide - (chips - 1) * CORES * per_dev * OBS_TILE
-    width = width_chip - per_dev * OBS_TILE
+    half_width = width_chip // 2
     rim_rows = RIM // 128
     obs_rows = obs // 128
     block = per_dev * cells
@@ -167,63 +168,106 @@
         for copy in halo(1):
             copy.start()
 
-    for t in range(per_dev):
-        state_copy(sibling, 0, t, me).start()
-    for j in range(1, chips):
-        p, far = across(j)
-        state_copy(p, far, 0, me).start()
-    for copy in own_copies:
-        copy.wait()
-
-    @pl.when(reg < regions - 1)
-    def _():
-        for copy in halo(0):
-            copy.wait_recv()
-
-    @pl.when(reg > 0)
-    def _():
-        for copy in halo(1):
-            copy.wait_recv()
-
-    def window(c):
-        return pw.at[:, pl.ds(pl.multiple_of(c * (CORES * per_dev * OBS_TILE), 128), width_chip)]
-
-    def yrows(m):
-        return yall.at[pl.ds(pl.multiple_of(m * rows, rows), rows), :]
-
-    def prior_copy(src, source, to, send_sem):
+    def begin(c, half):
+        inner = 1 - (2 * c) // chips
+        return (inner if half == 0 else 1 - inner) * half_width
+
+    def window(c, half):
+        at = c * (CORES * per_dev * OBS_TILE) + begin(c, half)
+        return pw.at[:, pl.ds(pl.multiple_of(at, 128), half_width)]
+
+    def yrows(m, half):
+        at = pl.multiple_of(begin(chip, half), 128)
+        return yall.at[pl.ds(pl.multiple_of(m * rows, rows), rows), pl.ds(at, half_width)]
+
+    def prior_copy(c, source, to, half, j):
+        at = pl.multiple_of(begin(c, half), 128)
         return pltpu.make_async_remote_copy(
-            src_ref=src,
-            dst_ref=yrows(source),
-            send_sem=send_sem,
-            recv_sem=yr_sem.at[source],
+            src_ref=window(c, half),
+            dst_ref=yall.at[pl.ds(pl.multiple_of(source * rows, rows), rows), pl.ds(at, half_width)],
+            send_sem=ys_sem.at[j, half],
+            recv_sem=yr_sem.at[source, half],
             device_id={"member": to},
             device_id_type=MESH,
         )
 
-    sends = []
-    for j in range(1, chips):
-        c = lax.rem(chip + j, chips)
-        sends.append(prior_copy(window(c), me, c * CORES + core, ys_sem.at[j]))
-    sends.append(prior_copy(window(chip), me, sibling, ys_sem.at[0]))
-    for copy in sends:
+    def forward_copy(source, half, j):
+        return pltpu.make_async_remote_copy(
+            src_ref=yrows(source, half),
+            dst_ref=yrows(source, half),
+            send_sem=fs_sem.at[j, half],
+            recv_sem=yr_sem.at[source, half],
+            device_id={"member": sibling},
+            device_id_type=MESH,
+        )
+
+    def own_prior(half):
+        return pltpu.make_async_copy(window(chip, half), yrows(me, half), loc_sem.at[6 + half])
+
+    def prior_sends(half):
+        made = []
+        for j in range(1, chips):
+            c = lax.rem(chip + j, chips)
+            made.append(prior_copy(c, me, c * CORES + core, half, j))
+        made.append(prior_copy(chip, me, sibling, half, 0))
+        return made
+
+    def forward(half):
+        for j in range(1, chips):
+            c = lax.rem(chip + j, chips)
+            source = c * CORES + core
+            forward_copy(source, half, j).wait_recv()
+            forward_copy(source, half, j).start()
+
+    def gathered(half):
+        own_prior(half).wait()
+        for j in range(chips):
+            c = lax.rem(chip + j, chips)
+            forward_copy(c * CORES + (CORES - 1 - core), half, j).wait_recv()
+
+    def other(j):
+        return lax.rem(chip + j, chips) * CORES + (CORES - 1 - core), CORES * j + 1
+
+    def start_state(t):
+        for j in range(1, chips):
+            for p, far in (across(j), other(j)):
+                state_copy(p, far, t, me).start()
+
+    for copy in own_copies:
+        copy.wait()
+    for copy in prior_sends(0):
         copy.start()
-    own_prior = pltpu.make_async_copy(window(chip), yrows(me), loc_sem.at[0])
-    own_prior.start()
-
-    pos0 = me * (per_dev * OBS_TILE)
-    nrow = width // 128
+    own_prior(0).start()
+    for t in range(per_dev):
+        state_copy(sibling, 0, t, me).start()
+
+    @pl.when(reg < regions - 1)
+    def _():
+        for copy in halo(0):
+            copy.wait_recv()
+
+    @pl.when(reg > 0)
+    def _():
+        for copy in halo(1):
+            copy.wait_recv()
+
+    for copy in prior_sends(1):
+        copy.start()
+    own_prior(1).start()
+
+    pos0 = chip * (CORES * per_dev * OBS_TILE)
+    nrow = width_chip // 128
     hpad = (nrow + 15) // 16 * 16
     slots = tobs.shape[1]
     first = me * per_dev
     lane = lax.broadcasted_iota(jnp.int32, (1, slots), 1)
     hi_iota = lax.broadcasted_iota(jnp.int32, (hpad, slots), 0)
     lo_iota = lax.broadcasted_iota(jnp.int32, (128, slots), 0)
-    base = per_dev * me
-    value_row = jnp.concatenate([vw[pl.ds(base + h, 1), :] for h in range(nrow)], axis=1)
+    base = chip * (CORES * per_dev * OBS_TILE // 128)
+    values[...] = jnp.concatenate([vw[pl.ds(base + h, 1), :] for h in range(nrow)], axis=1)
     rinv_row = jnp.concatenate([rw[pl.ds(base + h, 1), :] for h in range(nrow)], axis=1)
-    place = lax.broadcasted_iota(jnp.int32, (1, width), 1)
-    weights = []
+    place = lax.broadcasted_iota(jnp.int32, (1, width_chip), 1)
+    centre0 = RIM + OBS_TILE // 2 + core * (per_dev * OBS_TILE)
     for t in range(per_dev):
         rel = tv[pl.ds(first + t, 1), :] - pos0
         live = lane < ts[first + t]
@@ -233,58 +277,56 @@
         one_lo = jnp.where(lo_iota == lo, 1.0, 0.0).astype(BF16)
         grid = mm_nt(one_hi, one_lo)
         mask = jnp.concatenate([grid[h : h + 1, :] for h in range(nrow)], axis=1)
-        dist = jnp.abs(place - (RIM + t * OBS_TILE + OBS_TILE // 2)).astype(F32) / LOC
-        weights.append(jnp.sqrt(mask * rinv_row / (1.0 + dist * dist)))
-
-    for j in range(1, chips):
-        c = lax.rem(chip + j, chips)
-        source = c * CORES + core
-        prior_copy(yrows(source), source, sibling, fs_sem.at[j]).wait_recv()
-        prior_copy(yrows(source), source, sibling, fs_sem.at[j]).start()
-    for copy in sends:
-        copy.wait_send()
-    def other(j):
-        return lax.rem(chip + j, chips) * CORES + (CORES - 1 - core), CORES * j + 1
-
-    for j in range(1, chips):
-        p, far = other(j)
-        state_copy(p, far, 0, me).start()
+        dist = jnp.abs(place - (centre0 + t * OBS_TILE)).astype(F32) / LOC
+        roots[t] = jnp.sqrt(mask * rinv_row / (1.0 + dist * dist))
+
+    chunk = 256
+    tiles = range(per_dev)
+
+    def perturb(half):
+        for k in range(half_width // chunk):
+            at = pl.ds(pl.multiple_of(begin(chip, half) + k * chunk, 128), chunk)
+            y = yall[:, at].astype(F32)
+            ybar = jnp.sum(y, axis=0, keepdims=True) * (1.0 / members)
+            pert = y - ybar
+            dep = values[:, at] - ybar
+            for t in tiles:
+                root = roots[t, :, at]
+                high, low = split(pert * root)
+                uh[t, :members, at] = high
+                ul[t, :, at] = low
+                scaled = jnp.broadcast_to(root * dep, (8, chunk))
+                rough = scaled.astype(BF16).astype(F32)
+                uh[t, members:, at] = jnp.concatenate([rough, scaled - rough], axis=0).astype(BF16)
+
+    def products(half):
+        at = pl.ds(pl.multiple_of(begin(chip, half), 128), half_width)
+        both = [uh[t, :, at] for t in tiles]
+        main = [mm_nt(both[t], both[t][:members]) for t in tiles]
+        return main, [mm_nt(both[t], ul[t, :, at]) for t in tiles]
+
+    forward(0)
+    gathered(0)
+    perturb(0)
+    for half in range(2):
+        for copy in prior_sends(half):
+            copy.wait_send()
+    start_state(0)
+    main, cross = products(0)
+    forward(1)
     for t in range(1, per_dev):
-        for j in range(1, chips):
-            for p, far in (across(j), other(j)):
-                state_copy(p, far, t, me).start()
-
-    for j in range(chips):
-        c = lax.rem(chip + j, chips)
-        source = c * CORES + (CORES - 1 - core)
-        prior_copy(yrows(source), source, sibling, fs_sem.at[0]).wait_recv()
-    own_prior.wait()
-
-    offset = core * (per_dev * OBS_TILE)
-    chunk = 256
-    for k in range(width // chunk):
-        at = slice(k * chunk, (k + 1) * chunk)
-        y = yall[:, pl.ds(pl.multiple_of(offset + k * chunk, 128), chunk)].astype(F32)
-        ybar = jnp.sum(y, axis=0, keepdims=True) * (1.0 / members)
-        pert = y - ybar
-        dep = value_row[:, at] - ybar
-        for t in range(per_dev):
-            root = weights[t][:, at]
-            high, low = split(pert * root)
-            uh[t, :members, at] = high
-            ul[t, :, at] = low
-            scaled = jnp.broadcast_to(root * dep, (8, chunk))
-            rough = scaled.astype(BF16).astype(F32)
-            uh[t, members:, at] = jnp.concatenate([rough, scaled - rough], axis=0).astype(BF16)
+        start_state(t)
+    gathered(1)
+    perturb(1)
+    more_main, more_cross = products(1)
+    main = [a + b for a, b in zip(main, more_main)]
+    cross = [a + b for a, b in zip(cross, more_cross)]
 
     row_i = lax.broadcasted_iota(jnp.int32, (members, members), 0)
     col_i = lax.broadcasted_iota(jnp.int32, (members, members), 1)
     eye = jnp.where(row_i == col_i, 1.0, 0.0).astype(F32)
-    tiles = range(per_dev)
     cs = factors(members)
     scales, ps, es, vs = [], [], [], []
-    main = [mm_nt(uh[t], uh[t, :members, :]) for t in tiles]
-    cross = [mm_nt(uh[t], ul[t]) for t in tiles]
     for t in tiles:
         half = cross[t][:members]
         amat = (members - 1.0) * eye + main[t][:members] + (half + half.T)
@@ -321,57 +363,56 @@
 
     own_state.wait()
 
-    def result_copy(p, j, t, sem_from):
+    def result_copy(p, j, n, source):
         return pltpu.make_async_remote_copy(
-            src_ref=res.at[pl.ds(pl.multiple_of(p * rows, rows), rows), pl.ds(t * cells, cells)],
-            dst_ref=out.at[:, pl.ds(pl.multiple_of(me * block + t * cells, 128), cells)],
-            send_sem=os_sem.at[j, t],
-            recv_sem=or_sem.at[sem_from, t],
+            src_ref=res.at[pl.ds(pl.multiple_of(p * rows, rows), rows), pl.ds(n * PIECE, PIECE)],
+            dst_ref=out.at[:, pl.ds(pl.multiple_of(me * block + n * PIECE, 128), PIECE)],
+            send_sem=os_sem.at[j, n],
+            recv_sem=or_sem.at[source, n],
             device_id={"member": p},
             device_id_type=MESH,
         )
 
-    def own_result(t):
+    def own_result(n):
         return pltpu.make_async_copy(
-            res.at[pl.ds(pl.multiple_of(me * rows, rows), rows), pl.ds(t * cells, cells)],
-            out.at[:, pl.ds(pl.multiple_of(me * block + t * cells, 128), cells)],
-            loc_sem.at[1 + t],
+            res.at[pl.ds(pl.multiple_of(me * rows, rows), rows), pl.ds(n * PIECE, PIECE)],
+            out.at[:, pl.ds(pl.multiple_of(me * block + n * PIECE, 128), PIECE)],
+            own_sem.at[n],
         )
 
-    for t in range(per_dev):
-        for j in range(1, groups):
-            p = peer(j)
-            state_copy(p, j, t, p).wait_recv()
-
-        def columns(n, carry):
-            at = pl.ds(pl.multiple_of(t * cells + n * chunk, 128), chunk)
+    pieces = block // PIECE
+    for n in range(pieces):
+        t = n * PIECE // cells
+        if n * PIECE % cells == 0:
+            for j in range(1, groups):
+                p = peer(j)
+                state_copy(p, j, t, p).wait_recv()
+        for k in range(PIECE // chunk):
+            at = slice(n * PIECE + k * chunk, n * PIECE + (k + 1) * chunk)
             x = xall[:, at].astype(F32)
             xbar = jnp.sum(x, axis=0, keepdims=True) * (1.0 / members)
             pert = (x - xbar).astype(BF16)
             res[:, at] = (xbar + mm(wt[t], pert)).astype(BF16)
-            return carry
-
-        lax.fori_loop(0, cells // chunk, columns, 0)
         for j in range(1, groups):
-            result_copy(peer(j), j, t, me).start()
-        own_result(t).start()
-
-    for t in range(per_dev):
-        own_result(t).wait()
-        for j in range(1, groups):
-            result_copy(peer(j), j, t, me).wait_send()
+            result_copy(peer(j), j, n, me).start()
+        own_result(n).start()
+
+    for n in range(pieces):
+        own_result(n).wait()
         for j in range(1, groups):
             p = peer(j)
-            result_copy(p, j, t, p).wait_recv()
+            result_copy(p, j, n, p).wait_recv()
+        for j in range(1, groups):
+            result_copy(peer(j), j, n, me).wait_send()
     for t in range(per_dev):
         state_copy(sibling, 0, t, me).wait_send()
         for j in range(1, chips):
             for p, far in (across(j), other(j)):
                 state_copy(p, far, t, me).wait_send()
-    for j in range(1, chips):
-        c = lax.rem(chip + j, chips)
-        source = c * CORES + core
-        prior_copy(yrows(source), source, sibling, fs_sem.at[j]).wait_send()
+    for half in range(2):
+        for j in range(1, chips):
+            c = lax.rem(chip + j, chips)
+            forward_copy(c * CORES + core, half, j).wait_send()
 
     @pl.when(reg > 0)
     def _():
@@ -393,7 +434,7 @@
     members = groups * rows
     chips = groups // CORES
     width_chip = obs + 2 * RIM - (chips - 1) * CORES * per_dev * OBS_TILE
-    width = width_chip - per_dev * OBS_TILE
+    pieces = per_dev * cells // PIECE
     sizes = (groups, regions, rows, per_dev, cells, obs)
     dma = pltpu.SemaphoreType.DMA
     return pl.pallas_call(
@@ -407,22 +448,25 @@
             pltpu.VMEM(((obs + 2 * RIM) // 128, 128), F32),
             pltpu.VMEM(tile_obs.shape, jnp.int32),
             pltpu.SMEM(tile_count.shape, jnp.int32),
+            pltpu.VMEM((per_dev, 1, width_chip), F32),
+            pltpu.VMEM((1, width_chip), F32),
             pltpu.VMEM((members, width_chip), BF16),
             pltpu.VMEM((members, per_dev * cells), BF16),
             pltpu.VMEM((members, per_dev * cells), BF16),
-            pltpu.VMEM((per_dev, members + 16, width), BF16),
-            pltpu.VMEM((per_dev, members, width), BF16),
+            pltpu.VMEM((per_dev, members + 16, width_chip), BF16),
+            pltpu.VMEM((per_dev, members, width_chip), BF16),
             pltpu.VMEM((per_dev, members, members), BF16),
+            dma((8,)),
+            dma((pieces,)),
             dma((6,)),
             dma((6,)),
-            dma((6,)),
-            dma((chips,)),
-            dma((groups,)),
-            dma((chips,)),
+            dma((chips, 2)),
+            dma((groups, 2)),
+            dma((chips, 2)),
             dma((groups, per_dev)),
             dma((groups, per_dev)),
-            dma((groups, per_dev)),
-            dma((groups, per_dev)),
+            dma((groups, pieces)),
+            dma((groups, pieces)),
         ],
         compiler_params=pltpu.CompilerParams(
             collective_id=0, has_side_effects=True, vmem_limit_bytes=62 * 1024 * 1024

time: 52.1 us -> 51.8 us (level)
    pallas_call x1, Pallas kernels: 49.3 us -> 48.8 us  [body(): pl.pallas_call(functools.partial(kernel, sizes), out_shape=jax.ShapeDtype...]
where the time goes in v2:
time: 51.8 us; the launch traced here: 51.4 us
  Pallas kernels  48.8 us (94%)
  local copies, waits for them, and re-layouts  2.65 us (5%)
    pallas_call x1, Pallas kernels, body(): pl.pallas_call(functools.partial(kernel, sizes), out_shape=jax.ShapeDtype...  48.8 us
    unnamed x1, local copies, waits for them, and re-layouts  2.65 us

profile of v2, /device:TPU:1, one launch (start us, length us, event | category | flops | bytes accessed | tf_op | source)
XLA Modules:
  0.0 51.4 jit_solution(280023992550930085)
XLA Ops:
  0.0 48.8 %shard_map.64 = bf16[32,24576]{1,0:T(8,128)(2,1)} custom-call(bf16[32,24576]{1,0:T(8,128)(2,1)} %state.1, bf16[32,2048]{1,0:T(8,128)(2,1)} %prior.1, f32[16,128]{1,0:T(8,128)} %bitcast.2, f32[16,128]{1,0:T(8,128)} %bitcast.3, s32[16,2048]{1,0:T(8,128)} %tobs.1, s32[16]{0:T(128)} %tcount.1), custom_call_target="tpu_custom_call" | custom-call | flops 4000000000 | bytes 8000000 | tf_op jit(solution)/shard_map/pallas_call | solution.py:440
  48.8 2.7 %copy.8 = bf16[32,24576]{1,0:T(8,128)(2,1)} copy(bf16[32,24576]{1,0:T(8,128)(2,1)} %shard_map.64) | data formatting | bytes 3145728

commit v3 on v2

--- a/solution.py
+++ b/solution.py
@@ -299,11 +299,10 @@
                 rough = scaled.astype(BF16).astype(F32)
                 uh[t, members:, at] = jnp.concatenate([rough, scaled - rough], axis=0).astype(BF16)
 
-    def products(half):
+    def products(t, half):
         at = pl.ds(pl.multiple_of(begin(chip, half), 128), half_width)
-        both = [uh[t, :, at] for t in tiles]
-        main = [mm_nt(both[t], both[t][:members]) for t in tiles]
-        return main, [mm_nt(both[t], ul[t, :, at]) for t in tiles]
+        both = uh[t, :, at]
+        return mm_nt(both, both[:members]), mm_nt(both, ul[t, :, at])
 
     forward(0)
     gathered(0)
@@ -312,56 +311,48 @@
         for copy in prior_sends(half):
             copy.wait_send()
     start_state(0)
-    main, cross = products(0)
+    early = [products(t, 0) for t in tiles]
     forward(1)
     for t in range(1, per_dev):
         start_state(t)
     gathered(1)
     perturb(1)
-    more_main, more_cross = products(1)
-    main = [a + b for a, b in zip(main, more_main)]
-    cross = [a + b for a, b in zip(cross, more_cross)]
 
     row_i = lax.broadcasted_iota(jnp.int32, (members, members), 0)
     col_i = lax.broadcasted_iota(jnp.int32, (members, members), 1)
     eye = jnp.where(row_i == col_i, 1.0, 0.0).astype(F32)
     cs = factors(members)
-    scales, ps, es, vs = [], [], [], []
-    for t in tiles:
-        half = cross[t][:members]
-        amat = (members - 1.0) * eye + main[t][:members] + (half + half.T)
+
+    def transform(t):
+        late = products(t, 1)
+        main, cross = early[t][0] + late[0], early[t][1] + late[1]
+        half = cross[:members]
+        amat = (members - 1.0) * eye + main[:members] + (half + half.T)
         mmat = amat * (1.0 / (members - 1.0))
         scale = jnp.sqrt(jnp.sum(jnp.sum(mmat * mmat, axis=0, keepdims=True), axis=1, keepdims=True))
-        rhs = main[t][members : members + 1] + main[t][members + 8 : members + 9] + cross[t][members : members + 1]
-        scales.append(scale)
-        ps.append(mmat / scale)
-        vs.append(jnp.broadcast_to(rhs * (float(np.prod(cs)) / (members - 1.0)) / scale, (16, members)))
-        es.append(eye - cs[0] * ps[t])
-
-    zs = [1.5 * eye - 0.5 * ps[t] for t in tiles]
-    squares = [None for t in tiles]
-    for level in range(max(len(cs), 2 * ITERS)):
-        for t in tiles:
+        rhs = main[members : members + 1] + main[members + 8 : members + 9] + cross[members : members + 1]
+        p = mmat / scale
+        v = jnp.broadcast_to(rhs * (float(np.prod(cs)) / (members - 1.0)) / scale, (16, members))
+        e = eye - cs[0] * p
+        z = 1.5 * eye - 0.5 * p
+        for level in range(max(len(cs), 2 * ITERS - 1)):
+            if level < len(cs):
+                e2, v2 = split(e), split(v)
             if level < len(cs) - 1:
-                e = split(es[t])
-                v = split(vs[t])
-                both = dot3(tuple(jnp.concatenate(x, axis=0) for x in zip(e, v)), e)
-                vs[t] = vs[t] + both[members:]
-                es[t] = (1.0 - cs[level + 1]) * eye + cs[level + 1] * both[:members]
+                both = dot3(tuple(jnp.concatenate(x, axis=0) for x in zip(e2, v2)), e2)
+                v = v + both[members:]
+                e = (1.0 - cs[level + 1]) * eye + cs[level + 1] * both[:members]
             elif level == len(cs) - 1:
-                vs[t] = vs[t] + dot3(split(vs[t]), split(es[t]))
+                v = v + dot3(v2, e2)
             if level < 2 * ITERS - 2:
                 if level % 2 == 0:
-                    p = split(ps[t])
-                    squares[t] = dot3(p, p)
+                    p2 = split(p)
+                    square = dot3(p2, p2)
                 else:
-                    ps[t] = 2.25 * ps[t] + dot3(split(squares[t]), split(0.25 * ps[t] - 1.5 * eye))
+                    p = 2.25 * p + dot3(split(square), split(0.25 * p - 1.5 * eye))
             if level >= 2 and level % 2 == 0 and level <= 2 * ITERS - 2:
-                zs[t] = dot3(split(zs[t]), split(1.5 * eye - 0.5 * ps[t]))
-    for t in tiles:
-        wt[t] = (zs[t] / jnp.sqrt(scales[t]) + vs[t][:1]).astype(BF16)
-
-    own_state.wait()
+                z = dot3(split(z), split(1.5 * eye - 0.5 * p))
+        wt[t] = (z / jnp.sqrt(scale) + v[:1]).astype(BF16)
 
     def result_copy(p, j, n, source):
         return pltpu.make_async_remote_copy(
@@ -384,6 +375,9 @@
     for n in range(pieces):
         t = n * PIECE // cells
         if n * PIECE % cells == 0:
+            transform(t)
+            if t == 0:
+                own_state.wait()
             for j in range(1, groups):
                 p = peer(j)
                 state_copy(p, j, t, p).wait_recv()
@@ -439,9 +433,9 @@
     dma = pltpu.SemaphoreType.DMA
     return pl.pallas_call(
         functools.partial(kernel, sizes),
-        out_shape=jax.ShapeDtypeStruct(state_prior.shape, state_prior.dtype),
+        out_shape=pltpu.VMEM(state_prior.shape, state_prior.dtype),
         in_specs=[pl.BlockSpec(memory_space=pl.ANY)] * 6,
-        out_specs=pl.BlockSpec(memory_space=pl.ANY),
+        out_specs=pl.BlockSpec(memory_space=pltpu.VMEM),
         scratch_shapes=[
             pltpu.VMEM((rows, obs + 2 * RIM), BF16),
             pltpu.VMEM(((obs + 2 * RIM) // 128, 128), F32),
@@ -469,7 +463,7 @@
             dma((groups, pieces)),
         ],
         compiler_params=pltpu.CompilerParams(
-            collective_id=0, has_side_effects=True, vmem_limit_bytes=62 * 1024 * 1024
+            collective_id=0, has_side_effects=True, vmem_limit_bytes=57 * 1024 * 1024
         ),
         cost_estimate=pl.CostEstimate(flops=4_000_000_000, bytes_accessed=8_000_000, transcendentals=0),
     )(

time: 51.8 us -> 50.2 us (0.969)
  local copies, waits for them, and re-layouts: 2.65 us -> 1.15 us
    unnamed x1, local copies, waits for them, and re-layouts: 2.65 us -> 1.15 us
where the time goes in v3:
time: 50.2 us; the launch traced here: 49.8 us
  Pallas kernels  48.7 us (97%)
  local copies, waits for them, and re-layouts  1.15 us (2%)
    pallas_call x1, Pallas kernels, body(): pl.pallas_call(functools.partial(kernel, sizes), out_shape=pltpu.VMEM(sta...  48.7 us
    unnamed x1, local copies, waits for them, and re-layouts  1.15 us

profile of v3, /device:TPU:1, one launch (start us, length us, event | category | flops | bytes accessed | tf_op | source)
XLA Modules:
  0.0 49.8 jit_solution(12201344694462381133)
XLA Ops:
  0.0 48.7 %shard_map.64 = bf16[32,24576]{1,0:T(8,128)(2,1)S(1)} custom-call(bf16[32,24576]{1,0:T(8,128)(2,1)} %state.1, bf16[32,2048]{1,0:T(8,128)(2,1)} %prior.1, f32[16,128]{1,0:T(8,128)} %bitcast.2, f32[16,128]{1,0:T(8,128)} %bitcast.3, s32[16,2048]{1,0:T(8,128)} %tobs.1, s32[16]{0:T(128)} %tcount.1), custom_call_target="tpu_custom_call" | custom-call | flops 4000000000 | bytes 8000000 | tf_op jit(solution)/shard_map/pallas_call | solution.py:434
  48.7 1.1 %copy.8 = bf16[32,24576]{1,0:T(8,128)(2,1)} copy(bf16[32,24576]{1,0:T(8,128)(2,1)S(1)} %shard_map.64) | data formatting | bytes 3145728

commit v4 on v3

--- a/solution.py
+++ b/solution.py
@@ -109,8 +109,18 @@
             device_id_type=MESH,
         )
 
+    def partner(j):
+        flips = []
+        for bit in range(max(chips - 1, 1).bit_length()):
+            size = 2**bit
+            flips.append(size * (1 - 2 * lax.rem(chip // size, 2)))
+        if j in (1, 2) and chips > 2:
+            one, two = (flips[0], flips[1]) if j == 1 else (flips[1], flips[0])
+            return chip + one * (1 - core) + two * core
+        return chip + sum(flips[bit] for bit in range(len(flips)) if j >> bit & 1)
+
     def across(j):
-        return lax.rem(chip + j, chips) * CORES + core, CORES * j
+        return partner(j) * CORES + core, CORES * j
 
     own_state = pltpu.make_async_copy(
         state.at[:, pl.ds(pl.multiple_of(me * block, 128), block)],
@@ -207,7 +217,7 @@
     def prior_sends(half):
         made = []
         for j in range(1, chips):
-            c = lax.rem(chip + j, chips)
+            c = partner(j)
             made.append(prior_copy(c, me, c * CORES + core, half, j))
         made.append(prior_copy(chip, me, sibling, half, 0))
         return made
@@ -226,11 +236,16 @@
             forward_copy(c * CORES + (CORES - 1 - core), half, j).wait_recv()
 
     def other(j):
-        return lax.rem(chip + j, chips) * CORES + (CORES - 1 - core), CORES * j + 1
+        return partner(j) * CORES + (CORES - 1 - core), CORES * j + 1
+
+    def others():
+        return [make(j) for j in range(1, chips) for make in (across, other)]
+
+    early_state = [across(j) for j in range(1, min(chips, 3))]
 
     def start_state(t):
-        for j in range(1, chips):
-            for p, far in (across(j), other(j)):
+        for p, far in others():
+            if t > 0 or far not in [place for _, place in early_state]:
                 state_copy(p, far, t, me).start()
 
     for copy in own_copies:
@@ -254,6 +269,8 @@
     for copy in prior_sends(1):
         copy.start()
     own_prior(1).start()
+    for p, far in early_state:
+        state_copy(p, far, 0, me).start()
 
     pos0 = chip * (CORES * per_dev * OBS_TILE)
     nrow = width_chip // 128
@@ -307,14 +324,13 @@
     forward(0)
     gathered(0)
     perturb(0)
+    forward(1)
+    for t in tiles:
+        start_state(t)
+    early = [products(t, 0) for t in tiles]
     for half in range(2):
         for copy in prior_sends(half):
             copy.wait_send()
-    start_state(0)
-    early = [products(t, 0) for t in tiles]
-    forward(1)
-    for t in range(1, per_dev):
-        start_state(t)
     gathered(1)
     perturb(1)
 
@@ -387,8 +403,8 @@
             xbar = jnp.sum(x, axis=0, keepdims=True) * (1.0 / members)
             pert = (x - xbar).astype(BF16)
             res[:, at] = (xbar + mm(wt[t], pert)).astype(BF16)
-        for j in range(1, groups):
-            result_copy(peer(j), j, n, me).start()
+        for p, far in [(sibling, 0)] + others():
+            result_copy(p, far, n, me).start()
         own_result(n).start()
 
     for n in range(pieces):
@@ -396,13 +412,12 @@
         for j in range(1, groups):
             p = peer(j)
             result_copy(p, j, n, p).wait_recv()
-        for j in range(1, groups):
-            result_copy(peer(j), j, n, me).wait_send()
+        for p, far in [(sibling, 0)] + others():
+            result_copy(p, far, n, me).wait_send()
     for t in range(per_dev):
         state_copy(sibling, 0, t, me).wait_send()
-        for j in range(1, chips):
-            for p, far in (across(j), other(j)):
-                state_copy(p, far, t, me).wait_send()
+        for p, far in others():
+            state_copy(p, far, t, me).wait_send()
     for half in range(2):
         for j in range(1, chips):
             c = lax.rem(chip + j, chips)

time: 50.2 us -> 49.6 us (0.988)
  Pallas kernels: 48.7 us -> 48 us
    pallas_call x1, Pallas kernels: 48.7 us -> 48 us  [body(): pl.pallas_call(functools.partial(kernel, sizes), out_shape=pltpu.VMEM(sta...]
where the time goes in v4:
time: 49.6 us; the launch traced here: 49.2 us
  Pallas kernels  48 us (97%)
  local copies, waits for them, and re-layouts  1.15 us (2%)
    pallas_call x1, Pallas kernels, body(): pl.pallas_call(functools.partial(kernel, sizes), out_shape=pltpu.VMEM(sta...  48 us
    unnamed x1, local copies, waits for them, and re-layouts  1.15 us

profile of v4, /device:TPU:1, one launch (start us, length us, event | category | flops | bytes accessed | tf_op | source)
XLA Modules:
  0.0 49.2 jit_solution(15667511662863767657)
XLA Ops:
  0.0 48.0 %shard_map.64 = bf16[32,24576]{1,0:T(8,128)(2,1)S(1)} custom-call(bf16[32,24576]{1,0:T(8,128)(2,1)} %state.1, bf16[32,2048]{1,0:T(8,128)(2,1)} %prior.1, f32[16,128]{1,0:T(8,128)} %bitcast.2, f32[16,128]{1,0:T(8,128)} %bitcast.3, s32[16,2048]{1,0:T(8,128)} %tobs.1, s32[16]{0:T(128)} %tcount.1), custom_call_target="tpu_custom_call" | custom-call | flops 4000000000 | bytes 8000000 | tf_op jit(solution)/shard_map/pallas_call | solution.py:449
  48.1 1.1 %copy.8 = bf16[32,24576]{1,0:T(8,128)(2,1)} copy(bf16[32,24576]{1,0:T(8,128)(2,1)S(1)} %shard_map.64) | data formatting | bytes 3145728

commit v5 on v4

--- a/solution.py
+++ b/solution.py
@@ -57,8 +57,8 @@
     sizes,
     state, prior, value, rinv, tobs, tcount,
     out,
-    pw, vw, rw, tv, ts, roots, values, yall, xall, res, uh, ul, wt,
-    loc_sem, own_sem, hs_sem, hr_sem, ys_sem, yr_sem, fs_sem, ss_sem, sr_sem, os_sem, or_sem,
+    vw, rw, tv, ts, roots, values, yall, xall, res, uh, ul, wt,
+    loc_sem, own_sem, hs_sem, hr_sem, ys_sem, yr_sem, fs_sem, zs_sem, ss_sem, sr_sem, os_sem, or_sem,
 ):
     groups, regions, rows, per_dev, cells, obs = sizes
     chips = groups // CORES
@@ -90,7 +90,9 @@
         pl.semaphore_signal(barrier, inc=1, device_id={"region": reg + 1}, device_id_type=MESH)
 
     own_copies = [
-        pltpu.make_async_copy(prior, pw.at[:, pl.ds(RIM, obs)], loc_sem.at[0]),
+        pltpu.make_async_copy(
+            prior, yall.at[pl.ds(pl.multiple_of(me * rows, rows), rows), pl.ds(RIM, obs)], loc_sem.at[0]
+        ),
         pltpu.make_async_copy(value, vw.at[pl.ds(rim_rows, obs_rows), :], loc_sem.at[1]),
         pltpu.make_async_copy(rinv, rw.at[pl.ds(rim_rows, obs_rows), :], loc_sem.at[2]),
         pltpu.make_async_copy(tobs, tv, loc_sem.at[4]),
@@ -131,13 +133,13 @@
 
     @pl.when(reg == 0)
     def _():
-        pw[:, :RIM] = jnp.zeros((rows, RIM), BF16)
+        yall[:, :RIM] = jnp.zeros((members, RIM), BF16)
         vw[:rim_rows, :] = jnp.zeros((rim_rows, 128), F32)
         rw[:rim_rows, :] = jnp.zeros((rim_rows, 128), F32)
 
     @pl.when(reg == regions - 1)
     def _():
-        pw[:, RIM + obs :] = jnp.zeros((rows, RIM), BF16)
+        yall[:, RIM + obs :] = jnp.zeros((members, RIM), BF16)
         vw[rim_rows + obs_rows :, :] = jnp.zeros((rim_rows, 128), F32)
         rw[rim_rows + obs_rows :, :] = jnp.zeros((rim_rows, 128), F32)
 
@@ -151,7 +153,6 @@
         made = []
         for n, (a, b) in enumerate(
             (
-                (prior.at[:, pl.ds(src, RIM)], pw.at[:, pl.ds(dst, RIM)]),
                 (value.at[pl.ds(src_row, rim_rows), :], vw.at[pl.ds(dst_row, rim_rows), :]),
                 (rinv.at[pl.ds(src_row, rim_rows), :], rw.at[pl.ds(dst_row, rim_rows), :]),
             )
@@ -160,8 +161,8 @@
                 pltpu.make_async_remote_copy(
                     src_ref=a,
                     dst_ref=b,
-                    send_sem=hs_sem.at[3 * side + n],
-                    recv_sem=hr_sem.at[3 * side + n],
+                    send_sem=hs_sem.at[2 * side + n],
+                    recv_sem=hr_sem.at[2 * side + n],
                     device_id={"region": at},
                     device_id_type=MESH,
                 )
@@ -178,62 +179,91 @@
         for copy in halo(1):
             copy.start()
 
+    bits = (chips - 1).bit_length()
+    orders = (list(range(bits)), list(range(bits))[::-1])
+    upper = (2 * chip) // chips
+    to_region = reg + 1 - 2 * upper
+    from_region = reg - 1 + 2 * upper
+    can_send = jnp.logical_and(to_region >= 0, to_region < regions)
+    can_receive = jnp.logical_and(from_region >= 0, from_region < regions)
+
+    def flipped(mask):
+        return chip + sum(
+            2**bit * (1 - 2 * lax.rem(chip // 2**bit, 2)) for bit in range(bits) if mask >> bit & 1
+        )
+
+    def member(mask):
+        return flipped(mask) * CORES + core
+
+    def yblock(m, part):
+        if part < 2:
+            columns = pl.ds(RIM + part * (obs // 2), obs // 2)
+        else:
+            columns = pl.ds(pl.multiple_of(upper * (RIM + obs), 128), RIM)
+        return yall.at[pl.ds(pl.multiple_of(m * rows, rows), rows), columns]
+
+    def prior_copy(m, part, send_sem, device):
+        return pltpu.make_async_remote_copy(
+            src_ref=yblock(m, part),
+            dst_ref=yblock(m, part),
+            send_sem=send_sem,
+            recv_sem=yr_sem.at[m, part],
+            device_id=device,
+            device_id_type=MESH,
+        )
+
+    def stage_copies(half, stage):
+        flip = 1 << orders[half][stage]
+        made = []
+        for mask in range(chips):
+            if not any(mask >> bit & 1 for bit in orders[half][stage:]):
+                made.append(prior_copy(member(mask), half, ys_sem.at[mask ^ flip, half], {"member": member(flip)}))
+        return made
+
+    def stage_masks(half, stage):
+        flip = 1 << orders[half][stage]
+        return [
+            mask for mask in range(chips)
+            if mask & flip and not any(mask >> bit & 1 for bit in orders[half][stage + 1 :])
+        ]
+
+    def forward_copy(mask, part):
+        return prior_copy(member(mask), part, fs_sem.at[mask, part], {"member": sibling})
+
+    def plane_copy(mask):
+        source = pl.ds(pl.multiple_of(obs + upper * (RIM - obs), 128), RIM)
+        m = member(mask)
+        return pltpu.make_async_remote_copy(
+            src_ref=yall.at[pl.ds(pl.multiple_of(m * rows, rows), rows), source],
+            dst_ref=yblock(m, 2),
+            send_sem=zs_sem.at[mask],
+            recv_sem=yr_sem.at[m, 2],
+            device_id={"region": to_region},
+            device_id_type=MESH,
+        )
+
+    def arrived(half, mask):
+        @pl.when(jnp.logical_and(can_send, upper == 1 - half))
+        def _():
+            plane_copy(mask).start()
+
+        forward_copy(mask, half).start()
+
+    def receive(half, stage):
+        for mask in stage_masks(half, stage):
+            forward_copy(mask, half).wait_recv()
+
+    def gathered():
+        for m in range(chips):
+            for half in range(2):
+                forward_copy_from(m, half).wait_recv()
+
+    def forward_copy_from(c, part):
+        return prior_copy(c * CORES + (CORES - 1 - core), part, fs_sem.at[0, part], {"member": sibling})
+
     def begin(c, half):
         inner = 1 - (2 * c) // chips
         return (inner if half == 0 else 1 - inner) * half_width
-
-    def window(c, half):
-        at = c * (CORES * per_dev * OBS_TILE) + begin(c, half)
-        return pw.at[:, pl.ds(pl.multiple_of(at, 128), half_width)]
-
-    def yrows(m, half):
-        at = pl.multiple_of(begin(chip, half), 128)
-        return yall.at[pl.ds(pl.multiple_of(m * rows, rows), rows), pl.ds(at, half_width)]
-
-    def prior_copy(c, source, to, half, j):
-        at = pl.multiple_of(begin(c, half), 128)
-        return pltpu.make_async_remote_copy(
-            src_ref=window(c, half),
-            dst_ref=yall.at[pl.ds(pl.multiple_of(source * rows, rows), rows), pl.ds(at, half_width)],
-            send_sem=ys_sem.at[j, half],
-            recv_sem=yr_sem.at[source, half],
-            device_id={"member": to},
-            device_id_type=MESH,
-        )
-
-    def forward_copy(source, half, j):
-        return pltpu.make_async_remote_copy(
-            src_ref=yrows(source, half),
-            dst_ref=yrows(source, half),
-            send_sem=fs_sem.at[j, half],
-            recv_sem=yr_sem.at[source, half],
-            device_id={"member": sibling},
-            device_id_type=MESH,
-        )
-
-    def own_prior(half):
-        return pltpu.make_async_copy(window(chip, half), yrows(me, half), loc_sem.at[6 + half])
-
-    def prior_sends(half):
-        made = []
-        for j in range(1, chips):
-            c = partner(j)
-            made.append(prior_copy(c, me, c * CORES + core, half, j))
-        made.append(prior_copy(chip, me, sibling, half, 0))
-        return made
-
-    def forward(half):
-        for j in range(1, chips):
-            c = lax.rem(chip + j, chips)
-            source = c * CORES + core
-            forward_copy(source, half, j).wait_recv()
-            forward_copy(source, half, j).start()
-
-    def gathered(half):
-        own_prior(half).wait()
-        for j in range(chips):
-            c = lax.rem(chip + j, chips)
-            forward_copy(c * CORES + (CORES - 1 - core), half, j).wait_recv()
 
     def other(j):
         return partner(j) * CORES + (CORES - 1 - core), CORES * j + 1
@@ -250,11 +280,22 @@
 
     for copy in own_copies:
         copy.wait()
-    for copy in prior_sends(0):
-        copy.start()
-    own_prior(0).start()
+    for half in range(2):
+        for copy in stage_copies(half, 0):
+            copy.start()
+    for half in range(2):
+        arrived(half, 0)
     for t in range(per_dev):
         state_copy(sibling, 0, t, me).start()
+    for stage in range(1, bits):
+        for half in range(2):
+            receive(half, stage - 1)
+            for copy in stage_copies(half, stage):
+                copy.start()
+            for mask in stage_masks(half, stage - 1):
+                arrived(half, mask)
+    for p, far in early_state:
+        state_copy(p, far, 0, me).start()
 
     @pl.when(reg < regions - 1)
     def _():
@@ -265,12 +306,6 @@
     def _():
         for copy in halo(1):
             copy.wait_recv()
-
-    for copy in prior_sends(1):
-        copy.start()
-    own_prior(1).start()
-    for p, far in early_state:
-        state_copy(p, far, 0, me).start()
 
     pos0 = chip * (CORES * per_dev * OBS_TILE)
     nrow = width_chip // 128
@@ -303,7 +338,7 @@
     def perturb(half):
         for k in range(half_width // chunk):
             at = pl.ds(pl.multiple_of(begin(chip, half) + k * chunk, 128), chunk)
-            y = yall[:, at].astype(F32)
+            y = yall[:, pl.ds(pl.multiple_of(pos0 + begin(chip, half) + k * chunk, 128), chunk)].astype(F32)
             ybar = jnp.sum(y, axis=0, keepdims=True) * (1.0 / members)
             pert = y - ybar
             dep = values[:, at] - ybar
@@ -321,17 +356,29 @@
         both = uh[t, :, at]
         return mm_nt(both, both[:members]), mm_nt(both, ul[t, :, at])
 
-    forward(0)
-    gathered(0)
+    for half in range(2):
+        receive(half, bits - 1)
+        for mask in stage_masks(half, bits - 1):
+            arrived(half, mask)
+    start_state(0)
+    gathered()
     perturb(0)
-    forward(1)
-    for t in tiles:
+
+    @pl.when(can_receive)
+    def _():
+        for mask in range(chips):
+            forward_copy(mask, 2).wait_recv()
+            forward_copy(mask, 2).start()
+
+    for t in range(1, per_dev):
         start_state(t)
     early = [products(t, 0) for t in tiles]
-    for half in range(2):
-        for copy in prior_sends(half):
-            copy.wait_send()
-    gathered(1)
+
+    @pl.when(can_receive)
+    def _():
+        for c in range(chips):
+            forward_copy_from(c, 2).wait_recv()
+
     perturb(1)
 
     row_i = lax.broadcasted_iota(jnp.int32, (members, members), 0)
@@ -419,9 +466,21 @@
         for p, far in others():
             state_copy(p, far, t, me).wait_send()
     for half in range(2):
-        for j in range(1, chips):
-            c = lax.rem(chip + j, chips)
-            forward_copy(c * CORES + core, half, j).wait_send()
+        for stage in range(bits):
+            for copy in stage_copies(half, stage):
+                copy.wait_send()
+        for mask in range(chips):
+            forward_copy(mask, half).wait_send()
+
+    @pl.when(can_send)
+    def _():
+        for mask in range(chips):
+            plane_copy(mask).wait_send()
+
+    @pl.when(can_receive)
+    def _():
+        for mask in range(chips):
+            forward_copy(mask, 2).wait_send()
 
     @pl.when(reg > 0)
     def _():
@@ -452,14 +511,13 @@
         in_specs=[pl.BlockSpec(memory_space=pl.ANY)] * 6,
         out_specs=pl.BlockSpec(memory_space=pltpu.VMEM),
         scratch_shapes=[
-            pltpu.VMEM((rows, obs + 2 * RIM), BF16),
             pltpu.VMEM(((obs + 2 * RIM) // 128, 128), F32),
             pltpu.VMEM(((obs + 2 * RIM) // 128, 128), F32),
             pltpu.VMEM(tile_obs.shape, jnp.int32),
             pltpu.SMEM(tile_count.shape, jnp.int32),
             pltpu.VMEM((per_dev, 1, width_chip), F32),
             pltpu.VMEM((1, width_chip), F32),
-            pltpu.VMEM((members, width_chip), BF16),
+            pltpu.VMEM((members, obs + 2 * RIM), BF16),
             pltpu.VMEM((members, per_dev * cells), BF16),
             pltpu.VMEM((members, per_dev * cells), BF16),
             pltpu.VMEM((per_dev, members + 16, width_chip), BF16),
@@ -467,11 +525,12 @@
             pltpu.VMEM((per_dev, members, members), BF16),
             dma((8,)),
             dma((pieces,)),
-            dma((6,)),
-            dma((6,)),
+            dma((4,)),
+            dma((4,)),
             dma((chips, 2)),
-            dma((groups, 2)),
-            dma((chips, 2)),
+            dma((groups, 3)),
+            dma((chips, 3)),
+            dma((chips,)),
             dma((groups, per_dev)),
             dma((groups, per_dev)),
             dma((groups, pieces)),

time: 49.6 us -> 48.1 us (0.970)
  Pallas kernels: 48 us -> 46.5 us
    pallas_call x1, Pallas kernels: 48 us -> 46.5 us  [body(): pl.pallas_call(functools.partial(kernel, sizes), out_shape=pltpu.VMEM(sta...]
where the time goes in v5:
time: 48.1 us; the launch traced here: 47.6 us
  Pallas kernels  46.5 us (97%)
  local copies, waits for them, and re-layouts  1.15 us (2%)
    pallas_call x1, Pallas kernels, body(): pl.pallas_call(functools.partial(kernel, sizes), out_shape=pltpu.VMEM(sta...  46.5 us
    unnamed x1, local copies, waits for them, and re-layouts  1.15 us

profile of v5, /device:TPU:1, one launch (start us, length us, event | category | flops | bytes accessed | tf_op | source)
XLA Modules:
  0.0 47.6 jit_solution(10528348814878458175)
XLA Ops:
  0.0 46.5 %shard_map.64 = bf16[32,24576]{1,0:T(8,128)(2,1)S(1)} custom-call(bf16[32,24576]{1,0:T(8,128)(2,1)} %state.1, bf16[32,2048]{1,0:T(8,128)(2,1)} %prior.1, f32[16,128]{1,0:T(8,128)} %bitcast.2, f32[16,128]{1,0:T(8,128)} %bitcast.3, s32[16,2048]{1,0:T(8,128)} %tobs.1, s32[16]{0:T(128)} %tcount.1), custom_call_target="tpu_custom_call" | custom-call | flops 4000000000 | bytes 8000000 | tf_op jit(solution)/shard_map/pallas_call | solution.py:508
  46.5 1.1 %copy.8 = bf16[32,24576]{1,0:T(8,128)(2,1)} copy(bf16[32,24576]{1,0:T(8,128)(2,1)S(1)} %shard_map.64) | data formatting | bytes 3145728

commit v6 on v5

--- a/solution.py
+++ b/solution.py
@@ -271,7 +271,7 @@
     def others():
         return [make(j) for j in range(1, chips) for make in (across, other)]
 
-    early_state = [across(j) for j in range(1, min(chips, 3))]
+    early_state = [make(j) for make in (across, other) for j in range(1, min(chips, 3))]
 
     def start_state(t):
         for p, far in others():
@@ -285,6 +285,8 @@
             copy.start()
     for half in range(2):
         arrived(half, 0)
+    for p, far in early_state[: len(early_state) // 2]:
+        state_copy(p, far, 0, me).start()
     for t in range(per_dev):
         state_copy(sibling, 0, t, me).start()
     for stage in range(1, bits):
@@ -294,7 +296,7 @@
                 copy.start()
             for mask in stage_masks(half, stage - 1):
                 arrived(half, mask)
-    for p, far in early_state:
+    for p, far in early_state[len(early_state) // 2 :]:
         state_copy(p, far, 0, me).start()
 
     @pl.when(reg < regions - 1)
@@ -386,7 +388,7 @@
     eye = jnp.where(row_i == col_i, 1.0, 0.0).astype(F32)
     cs = factors(members)
 
-    def transform(t):
+    def transform(t, between):
         late = products(t, 1)
         main, cross = early[t][0] + late[0], early[t][1] + late[1]
         half = cross[:members]
@@ -415,6 +417,8 @@
                     p = 2.25 * p + dot3(split(square), split(0.25 * p - 1.5 * eye))
             if level >= 2 and level % 2 == 0 and level <= 2 * ITERS - 2:
                 z = dot3(split(z), split(1.5 * eye - 0.5 * p))
+            for work in between.get(level, ()):
+                work()
         wt[t] = (z / jnp.sqrt(scale) + v[:1]).astype(BF16)
 
     def result_copy(p, j, n, source):
@@ -435,24 +439,35 @@
         )
 
     pieces = block // PIECE
-    for n in range(pieces):
-        t = n * PIECE // cells
-        if n * PIECE % cells == 0:
-            transform(t)
-            if t == 0:
-                own_state.wait()
-            for j in range(1, groups):
-                p = peer(j)
-                state_copy(p, j, t, p).wait_recv()
+    tile_pieces = cells // PIECE
+
+    def analysis(n):
         for k in range(PIECE // chunk):
             at = slice(n * PIECE + k * chunk, n * PIECE + (k + 1) * chunk)
             x = xall[:, at].astype(F32)
             xbar = jnp.sum(x, axis=0, keepdims=True) * (1.0 / members)
             pert = (x - xbar).astype(BF16)
-            res[:, at] = (xbar + mm(wt[t], pert)).astype(BF16)
-        for p, far in [(sibling, 0)] + others():
+            res[:, at] = (xbar + mm(wt[n // tile_pieces], pert)).astype(BF16)
+        for p, far in others() + [(sibling, 0)]:
             result_copy(p, far, n, me).start()
         own_result(n).start()
+
+    waiting = {}
+    for t in range(per_dev):
+        transform(t, waiting)
+        if t == 0:
+            own_state.wait()
+        for j in range(1, groups):
+            p = peer(j)
+            state_copy(p, j, t, p).wait_recv()
+        first_piece = t * tile_pieces
+        analysis(first_piece)
+        later = range(first_piece + 1, first_piece + tile_pieces)
+        if t == per_dev - 1:
+            for n in later:
+                analysis(n)
+        else:
+            waiting = {1 + 3 * i: [functools.partial(analysis, n)] for i, n in enumerate(later)}
 
     for n in range(pieces):
         own_result(n).wait()

time: 48.1 us -> 46.8 us (0.973)
  Pallas kernels: 46.5 us -> 45.2 us
    pallas_call x1, Pallas kernels: 46.5 us -> 45.2 us  [body(): pl.pallas_call(functools.partial(kernel, sizes), out_shape=pltpu.VMEM(sta...]
where the time goes in v6:
time: 46.8 us; the launch traced here: 46.3 us
  Pallas kernels  45.2 us (97%)
  local copies, waits for them, and re-layouts  1.15 us (2%)
    pallas_call x1, Pallas kernels, body(): pl.pallas_call(functools.partial(kernel, sizes), out_shape=pltpu.VMEM(sta...  45.2 us
    unnamed x1, local copies, waits for them, and re-layouts  1.15 us

profile of v6, /device:TPU:1, one launch (start us, length us, event | category | flops | bytes accessed | tf_op | source)
XLA Modules:
  0.0 46.3 jit_solution(10094242746758566796)
XLA Ops:
  0.0 45.2 %shard_map.64 = bf16[32,24576]{1,0:T(8,128)(2,1)S(1)} custom-call(bf16[32,24576]{1,0:T(8,128)(2,1)} %state.1, bf16[32,2048]{1,0:T(8,128)(2,1)} %prior.1, f32[16,128]{1,0:T(8,128)} %bitcast.2, f32[16,128]{1,0:T(8,128)} %bitcast.3, s32[16,2048]{1,0:T(8,128)} %tobs.1, s32[16]{0:T(128)} %tcount.1), custom_call_target="tpu_custom_call" | custom-call | flops 4000000000 | bytes 8000000 | tf_op jit(solution)/shard_map/pallas_call | solution.py:523
  45.2 1.1 %copy.8 = bf16[32,24576]{1,0:T(8,128)(2,1)} copy(bf16[32,24576]{1,0:T(8,128)(2,1)S(1)} %shard_map.64) | data formatting | bytes 3145728
